TPU v7x, 128 devices: a whole 4x4x4 slice. The times are simulated.
128 devices in a mesh: dp: 16 (over z_hi, x, core), tensor: 8 (over y, z_lo).
Axes of the slice: x: 4, y: 4, z: 4 (z_hi: 2, z_lo: 2; z = z_hi * 2 + z_lo), core: 2. Of those that a mesh axis runs over, the one named last changes fastest.
Arguments:
- train_hidden: bfloat16 [32768, 28672], P('dp', 'tensor'), may hold values from -6 to 6
- train_grad: bfloat16 [32768, 8192], P('dp', 'tensor'), may hold values from -6 to 6
- val_hidden: bfloat16 [1024, 28672], P('dp', 'tensor'), may hold values from -6 to 6
- val_grad: bfloat16 [1024, 8192], P('dp', 'tensor'), may hold values from -6 to 6
- seq_ids: int32 [16, 2048], P('dp'), may hold values from 0 to 7, never falling along the last dimension, each value on 1 to 1024 neighbouring positions
Outputs:
- seq_scores: float32 [128], P('dp')
- val_scores: float32 [1024], replicated
Inputs may be any that keep to these rules, and one draw needn't show every extreme that they name: Each row of seq_ids does not decrease, names every number 0 to 7, and no number more than 1024 times.
All inputs are finite; a program needn't handle non-finite values.
Results may differ from a plain program's by a relative error of at most 0.0003.
Values may be sent and summed in bfloat16 or wider, within the bound.
No kernel may reach another device: no remote copies, remote signals or barrier semaphores. Data moves between devices by JAX's collectives and lax.ppermute only.
A program may use at most 128 MiB of HBM per device.

v0:
```python
import jax
import jax.numpy as jnp
import numpy as np
from jax import lax
from jax.experimental import pallas as pl
from jax.experimental.pallas import tpu as pltpu
from jax.sharding import PartitionSpec as P

D = 8192
FF = 28672
TOK_DEV = 2048
SEQ_DEV = 8
VAL = 1024

DP = 16
TENSOR = 8
VAL_DEV = VAL // DP
LEAF = TOK_DEV // TENSOR
WAVE = VAL // 2
HIDDEN_DEV = FF // TENSOR
GRAD_DEV = D // TENSOR
GROUP = 64
BIAS = 100.0
MANTISSA = 16383.0


def along_z(d):
    return (d + 8) % 16


def along_core(d):
    return d ^ 1


def move_x(d, fn):
    z, x, core = d // 8, d // 2 % 4, d % 2
    return z * 8 + fn(x) * 2 + core


def first_x(d):
    return move_x(d, lambda x: x ^ 1 if d % 2 == 0 else 3 - x)


def second_x(d):
    return move_x(d, lambda x: 3 - x if d % 2 == 0 else x ^ 1)


def along_link(t, link):
    y, z = t // 2, t % 2
    if link == 0:
        return (y ^ 1) * 2 + z
    if link == 1:
        return (3 - y) * 2 + z
    return t ^ 1


LINK_OF_BIT = ((0, 1, 2), (1, 0, 2))


def send_dp(x, fn):
    return lax.ppermute(x, "dp", [(d, fn(d)) for d in range(DP)])


def send_link(x, bit):
    pairs = []
    for d in range(DP):
        link = LINK_OF_BIT[d % 2][bit]
        for t in range(TENSOR):
            pairs.append((d * TENSOR + t, d * TENSOR + along_link(t, link)))
    return lax.ppermute(x, ("dp", "tensor"), pairs)


def send_wrap(x):
    pairs = []
    for d in range(DP):
        for t in range(TENSOR):
            pairs.append((d * TENSOR + t, along_z(d) * TENSOR + (t ^ 1)))
    return lax.ppermute(x, ("dp", "tensor"), pairs)


def encode(x):
    a = x.reshape(8, 8, x.shape[-1])
    top = jnp.max(jnp.abs(a), axis=0)
    e = jnp.clip(jnp.floor(jnp.log2(jnp.maximum(top, 1e-26)) + 1.0002), -90.0, 120.0)
    inv = jnp.exp2(-e) * MANTISSA
    code = (e + BIAS).astype(jnp.int32)
    q = jnp.floor(a * inv[None] + 0.5).astype(jnp.int32) * 2
    bits = jnp.stack([(code >> i) & 1 for i in range(8)])
    return (q + bits).reshape(x.shape).astype(jnp.int16)


def decode(c):
    c = c.astype(jnp.int32).reshape(8, 8, c.shape[-1])
    low = c & 1
    code = low[0]
    for i in range(1, 8):
        code = code | (low[i] << i)
    s = jnp.exp2(code.astype(jnp.float32) - BIAS) * (1.0 / MANTISSA)
    return ((c >> 1).astype(jnp.float32) * s[None]).reshape(GROUP, c.shape[-1])


IN_VMEM = pl.BlockSpec(memory_space=pltpu.VMEM)
IN_SMEM = pl.BlockSpec(memory_space=pltpu.SMEM)
BRIEF = pl.CostEstimate(flops=1, bytes_accessed=1, transcendentals=0)


def vmem(x):
    return pltpu.with_memory_space_constraint(x, pltpu.VMEM)


def params(mib):
    return pltpu.CompilerParams(vmem_limit_bytes=mib * 1024 * 1024)


def part(start, size):
    if isinstance(start, int):
        return pl.ds(start, size)
    return pl.ds(pl.multiple_of(start, size), size)


def join(arrays):
    rows = [a.shape[0] for a in arrays]
    n = arrays[0].shape[1]

    def kernel(*refs):
        to = 0
        for ref, size in zip(refs[:-1], rows):
            refs[-1][to : to + size] = ref[...]
            to += size

    return pl.pallas_call(
        kernel,
        out_shape=pltpu.VMEM((sum(rows), n), arrays[0].dtype),
        in_specs=[IN_VMEM] * len(arrays),
        out_specs=IN_VMEM,
        compiler_params=params(4),
        cost_estimate=BRIEF,
        name="join",
    )(*[vmem(a) for a in arrays])


def beside(hidden, grad):
    def kernel(hidden_ref, grad_ref, out_ref):
        out_ref[:, :HIDDEN_DEV] = hidden_ref[...]
        out_ref[:, HIDDEN_DEV:] = grad_ref[...]

    return pl.pallas_call(
        kernel,
        out_shape=pltpu.VMEM((VAL_DEV, HIDDEN_DEV + GRAD_DEV), hidden.dtype),
        in_specs=[IN_VMEM, IN_VMEM],
        out_specs=IN_VMEM,
        compiler_params=params(4),
        cost_estimate=BRIEF,
        name="beside",
    )(vmem(hidden), vmem(grad))


def tie(x, after):
    return lax.optimization_barrier((x, after))[0]


def pieces(rows, count, fn):
    size = rows.shape[0] // count
    return [send_dp(rows[i * size : (i + 1) * size], fn) for i in range(count)]


def both_cores(twice):
    groups = [[d, d + 1] for d in range(0, DP, 2)]
    return lax.all_to_all(twice, "dp", 0, 0, axis_index_groups=groups, tiled=True)


def column_order(d):
    order = []
    for far in (False, True):
        near_part, other_part = [], []
        for e, held in ((d, near_part), (along_core(d), other_part)):
            e = along_z(e) if far else e
            held += [e, first_x(e), second_x(e), first_x(second_x(e))]
        rest = (near_part[2:], other_part[2:])
        rest = rest[:: -1 if far and d % 2 else 1]
        order += near_part[:2] + other_part[:2] + rest[0] + rest[1]
    return order


def tiles(m, n):
    for r in range(0, m, GROUP):
        for c in range(0, n, 128):
            yield r, c


def gram(scalars, x, y, bit, away):
    n, k = y.shape[0], x.shape[1]
    columns = slice(0, HIDDEN_DEV) if k == HIDDEN_DEV else slice(HIDDEN_DEV, HIDDEN_DEV + GRAD_DEV)
    rows = TOK_DEV // 2
    low = 2 - bit

    def kernel(s_ref, x_ref, y_ref, o_ref, acc):
        side = 1 - s_ref[bit] if away else s_ref[bit]
        blocks = TENSOR // 2
        for i in range(blocks + away):
            if i < blocks:
                block = (i >> low << (low + 1)) + (side << low) + (i & ((1 << low) - 1))
                to = acc.at[i % 2] if away else o_ref.at[i * LEAF : (i + 1) * LEAF]
                to[...] = lax.dot_general(
                    x_ref[part(block * LEAF, LEAF)],
                    y_ref[:, columns],
                    (((1,), (1,)), ((), ())),
                    preferred_element_type=jnp.float32,
                )
            if away and i > 0:
                for r, c in tiles(LEAF, n):
                    o_ref[(i - 1) * LEAF + r : (i - 1) * LEAF + r + GROUP, c : c + 128] = encode(
                        acc[(i - 1) % 2, r : r + GROUP, c : c + 128]
                    )

    return pl.pallas_call(
        kernel,
        out_shape=pltpu.VMEM((rows, n), jnp.int16 if away else jnp.float32),
        in_specs=[IN_SMEM, IN_VMEM, IN_VMEM],
        out_specs=IN_VMEM,
        scratch_shapes=[pltpu.VMEM((2, LEAF, n), jnp.float32)] if away else [pltpu.VMEM((8, 128), jnp.float32)],
        compiler_params=params(4),
        cost_estimate=BRIEF,
        name="gram",
    )(scalars, vmem(x), vmem(y))


def fold(scalars, kept, arrived, bit):
    rows, n = kept.shape
    half = rows // 2

    def kernel(s_ref, kept_ref, in_ref, send_ref, out_ref):
        keep = s_ref[bit]

        @pl.loop(0, half // GROUP)
        def _(r):
            away = part((1 - keep) * half + r * GROUP, GROUP)
            stay = part(keep * half + r * GROUP, GROUP)
            to = part(r * GROUP, GROUP)
            for c in range(0, n, 128):
                c = slice(c, c + 128)
                send_ref[to, c] = encode(kept_ref[away, c] + decode(in_ref[away, c]))
                out_ref[to, c] = kept_ref[stay, c] + decode(in_ref[stay, c])

    return pl.pallas_call(
        kernel,
        out_shape=(pltpu.VMEM((half, n), jnp.int16), pltpu.VMEM((half, n), jnp.float32)),
        in_specs=[IN_SMEM, IN_VMEM, IN_VMEM],
        out_specs=(IN_VMEM, IN_VMEM),
        compiler_params=params(4),
        cost_estimate=BRIEF,
        name="fold",
    )(scalars, vmem(kept), vmem(arrived))


def finish(scalars, act, act_in, grad, grad_in, ids):
    def kernel(s_ref, a_ref, ai_ref, g_ref, gi_ref, ids_ref, col_ref, seq_ref):
        lane = lax.broadcasted_iota(jnp.int32, (GROUP, 128), 1)
        seq = jnp.zeros((1, 128), jnp.float32)
        cols = [jnp.zeros((1, 128), jnp.float32) for _ in range(WAVE // 128)]
        leaf = 4 * s_ref[0] + 2 * s_ref[1] + s_ref[2]
        ids = ids_ref[...]
        first = jnp.zeros((1, 128), jnp.int32)
        past = jnp.zeros((1, 128), jnp.int32)
        for q in range(SEQ_DEV):
            first = jnp.where(lane[:1] == q, jnp.sum((ids < q).astype(jnp.int32), axis=1, keepdims=True), first)
            past = jnp.where(lane[:1] == q, jnp.sum((ids <= q).astype(jnp.int32), axis=1, keepdims=True), past)
        for r in range(0, LEAF, GROUP):
            rows = slice(r, r + GROUP)
            wide = jnp.zeros((GROUP, 128), jnp.float32)
            for j in range(WAVE // 128):
                c = slice(j * 128, j * 128 + 128)
                ghost = (a_ref[rows, c] + decode(ai_ref[rows, c])) * (g_ref[rows, c] + decode(gi_ref[rows, c]))
                wide = wide + ghost
                cols[j] = cols[j] + jnp.sum(ghost, axis=0, keepdims=True)
            total = jnp.sum(wide, axis=1, keepdims=True)
            token = leaf * LEAF + r + lax.broadcasted_iota(jnp.int32, (GROUP, 128), 0)
            mine = (token >= first) & (token < past)
            seq = seq + jnp.sum(jnp.where(mine, total, 0.0), axis=0, keepdims=True)
        for j in range(WAVE // 128):
            col_ref[:, j * 128 : j * 128 + 128] = cols[j]
        seq_ref[...] = seq

    return pl.pallas_call(
        kernel,
        out_shape=(pltpu.VMEM((1, WAVE), jnp.float32), pltpu.VMEM((1, 128), jnp.float32)),
        in_specs=[IN_SMEM] + [IN_VMEM] * 5,
        out_specs=(IN_VMEM, IN_VMEM),
        compiler_params=params(4),
        cost_estimate=BRIEF,
        name="finish",
    )(scalars, vmem(act), vmem(act_in), vmem(grad), vmem(grad_in), vmem(ids))


def scalar_table():
    table = []
    for d in range(DP):
        for t in range(TENSOR):
            side = ((t // 2 + 1) // 2 % 2, t // 4, t % 2)
            table.append([side[link] for link in LINK_OF_BIT[d % 2]] + [0] + column_order(d))
    return np.array(table, np.int32)


def local(train_hidden, train_grad, val_hidden, val_grad, seq_ids):
    device = lax.axis_index(("dp", "tensor"))
    scalars = lax.dynamic_index_in_dim(jnp.asarray(scalar_table()), device, keepdims=False)
    scalars, val_hidden, val_grad = lax.optimization_barrier((scalars, val_hidden, val_grad))
    last = [scalars]

    def after(x):
        return tie(x, last[0])

    def ordered(x):
        last[0] = x
        return x

    def joined(*arrays):
        return ordered(join([after(arrays[0]), *arrays[1:]]))

    def send_half(x, vals, bit):
        send = ordered(gram(scalars, x, after(vals), bit, True))
        return send_link(send, bit)

    def keep_half(x, vals, bit):
        return ordered(gram(scalars, x, after(vals), bit, False))

    def folded(kept, arrived, bit):
        send, kept = fold(scalars, after(kept), arrived, bit)
        ordered(kept)
        return kept, send_link(send, bit)

    own = ordered(beside(after(val_hidden), val_grad))
    near1 = send_dp(own, first_x)
    far0 = send_dp(own, along_z)
    near_pair = joined(own, near1)
    near2 = pieces(near_pair, 2, second_x)
    near_c1 = pieces(near_pair, 2, along_core)
    far0 = joined(far0)
    near_half = joined(near_pair, *near_c1)
    near2 = joined(*near2)
    near_c2 = pieces(near2, 4, along_core)
    far1 = send_dp(after(far0), first_x)
    near = joined(near_half, near2, *near_c2)

    act0_in = send_half(train_hidden, near, 0)
    far_pair = joined(far0, far1)
    far2 = send_dp(far_pair, second_x)
    far_c1 = send_dp(far_pair, along_core)
    grad0_in = send_half(train_grad, near, 2)
    far_half = joined(far_pair, far_c1)
    act0 = keep_half(train_hidden, near, 0)
    grad0 = keep_half(train_grad, near, 2)
    far_rest = both_cores(joined(far2, far2))
    act0, act0_in = folded(act0, act0_in, 1)
    far = joined(far_half, far_rest)
    act1_in = send_half(train_hidden, far, 0)
    grad1_in = send_half(train_grad, far, 2)
    grad0, grad0_in = folded(grad0, grad0_in, 0)
    act1 = keep_half(train_hidden, far, 0)
    grad1 = keep_half(train_grad, far, 2)
    act1, act1_in = folded(act1, act1_in, 1)
    grad1, grad1_in = folded(grad1, grad1_in, 0)
    act0, act0_in = folded(act0, act0_in, 2)
    grad0, grad0_in = folded(grad0, grad0_in, 1)
    act1, act1_in = folded(act1, act1_in, 2)
    grad1, grad1_in = folded(grad1, grad1_in, 1)
    col0, seq0 = finish(scalars, after(act0), act0_in, grad0, grad0_in, seq_ids)
    ordered(col0)
    col1, seq1 = finish(scalars, after(act1), act1_in, grad1, grad1_in, seq_ids)

    ours = (scalars[None, 4:] == jnp.arange(DP, dtype=jnp.int32)[:, None])[:, :, None].astype(jnp.float32)
    col = jnp.concatenate([col0, col1], axis=1).reshape(1, DP, VAL_DEV)
    col = jnp.sum(ours * col, axis=1).reshape(8, 128)
    total = jnp.concatenate([col, seq0 + seq1], axis=0)
    for link in range(3):
        total = total + lax.ppermute(total, "tensor", [(i, along_link(i, link)) for i in range(TENSOR)])
    segment = total[8, :SEQ_DEV]
    total = total[:8]
    for fn in (first_x, second_x):
        total = total + send_dp(total, fn)
    total = total + send_wrap(total)
    total = total + send_dp(total, along_core)
    seq_scale = 1.0 / (float(FF) * D * VAL * TOK_DEV) ** 0.5
    val_scale = 1.0 / (float(FF) * D * TOK_DEV * DP) ** 0.5
    return (segment * seq_scale, total.reshape(VAL) * val_scale)


def solution(mesh):
    in_specs = (
        P("dp", "tensor"),
        P("dp", "tensor"),
        P("dp", "tensor"),
        P("dp", "tensor"),
        P("dp", None),
    )
    out_specs = (P("dp"), P())
    return jax.shard_map(local, mesh=mesh, in_specs=in_specs, out_specs=out_specs, check_vma=False)
```

profile of v0, /device:TPU:1, one launch (start us, length us, event | category | flops | bytes accessed | tf_op | source)
XLA Modules:
  0.0 155.8 jit_solution(12881245059510681951)
XLA Ops:
  3.3 3.4 %collective-permute-start = (bf16[64,4608]{1,0:T(8,128)(2,1)S(1)}, bf16[64,4608]{1,0:T(8,128)(2,1)S(1)}, u32[]{:S(2)}, u32[]{:S(2)}) collective-permute-start(bf16[64,4608]{1,0:T(8,128)(2,1)S(1)} %beside.1.refs_0_), channel_id=1, source_target_pairs={{0,16},{8,56},{16,0},{24,40},{32,48},{40,24},{48,32},{56,8},{64,80... | collective-permute-start | bytes 1769480 | tf_op jit(solution)/shard_map/ppermute | solution.py:61
  6.7 3.6 %collective-permute-start.1 = (bf16[64,4608]{1,0:T(8,128)(2,1)S(1)}, bf16[64,4608]{1,0:T(8,128)(2,1)S(1)}, u32[]{:S(2)}, u32[]{:S(2)}) collective-permute-start(bf16[64,4608]{1,0:T(8,128)(2,1)S(1)} %beside.1.refs_0_), channel_id=1, source_target_pairs={{0,64},{8,72},{16,80},{24,88},{32,96},{40,104},{48,112},{56,120},{... | collective-permute-start | bytes 1769480 | tf_op jit(solution)/shard_map/ppermute | solution.py:61
  10.3 4.0 %collective-permute-done.refs_1_ = bf16[64,4608]{1,0:T(8,128)(2,1)S(1)} collective-permute-done((bf16[64,4608]{1,0:T(8,128)(2,1)S(1)}, bf16[64,4608]{1,0:T(8,128)(2,1)S(1)}, u32[]{:S(2)}, u32[]{:S(2)}) %collective-permute-start) | collective-permute-done | bytes 589856 | tf_op jit(solution)/shard_map/ppermute | solution.py:61
  16.5 7.4 %collective-permute-done.1.refs_0_ = bf16[64,4608]{1,0:T(8,128)(2,1)S(1)} collective-permute-done((bf16[64,4608]{1,0:T(8,128)(2,1)S(1)}, bf16[64,4608]{1,0:T(8,128)(2,1)S(1)}, u32[]{:S(2)}, u32[]{:S(2)}) %collective-permute-start.1) | collective-permute-done | bytes 589856 | tf_op jit(solution)/shard_map/ppermute | solution.py:61
  24.1 6.2 %collective-permute-done.5.refs_1_ = bf16[64,4608]{1,0:T(8,128)(2,1)S(1)} collective-permute-done((bf16[64,4608]{1,0:T(8,128)(2,1)S(1)}, bf16[64,4608]{1,0:T(8,128)(2,1)S(1)}, u32[]{:S(2)}, u32[]{:S(2)}) %collective-permute-start.5) | collective-permute-done | bytes 589856 | tf_op jit(solution)/shard_map/ppermute | solution.py:61
  30.5 2.7 %collective-permute-start.10 = (bf16[64,4608]{1,0:T(8,128)(2,1)S(1)}, bf16[64,4608]{1,0:T(8,128)(2,1)S(1)}, u32[]{:S(2)}, u32[]{:S(2)}) collective-permute-start(bf16[64,4608]{1,0:T(8,128)(2,1)S(1)} %join.10.refs_0_), channel_id=1, source_target_pairs={{0,16},{8,56},{16,0},{24,40},{32,48},{40,24},{48,32},{56,8},{64,80... | collective-permute-start | bytes 1769480 | tf_op jit(solution)/shard_map/ppermute | solution.py:61
  36.5 5.0 %gram.8 = s16[1024,512]{1,0:T(8,128)(2,1)S(1)} custom-call(s32[20]{0:T(128)S(1)} %dynamic-slice_bitcast_fusion.s_ref, bf16[2048,3584]{1,0:T(8,128)(2,1)S(1)} %copy-done, bf16[512,4608]{1,0:T(8,128)(2,1)S(1)} %join.13.y_ref), custom_call_target="tpu_custom_call" | custom-call | flops 1 | bytes 1 | tf_op jit(solution)/shard_map/gram/pallas_call | solution.py:216
  43.3 2.8 %collective-permute-start.13 = (s16[1024,512]{1,0:T(8,128)(2,1)S(1)}, s16[1024,512]{1,0:T(8,128)(2,1)S(1)}, u32[]{:S(2)}, u32[]{:S(2)}) collective-permute-start(s16[1024,512]{1,0:T(8,128)(2,1)S(1)} %gram.8), channel_id=1, source_target_pairs={{0,2},{1,3},{2,0},{3,1},{4,6},{5,7},{6,4},{7,5},{8,14},{9,15},{10,... | collective-permute-start | bytes 3145736 | tf_op jit(solution)/shard_map/ppermute | solution.py:70
  46.1 2.5 %gram.9 = s16[1024,512]{1,0:T(8,128)(2,1)S(1)} custom-call(s32[20]{0:T(128)S(1)} %dynamic-slice_bitcast_fusion.s_ref, bf16[2048,1024]{1,0:T(8,128)(2,1)S(1)} %copy-done.1, bf16[512,4608]{1,0:T(8,128)(2,1)S(1)} %join.13.y_ref), custom_call_target="tpu_custom_call" | custom-call | flops 1 | bytes 1 | tf_op jit(solution)/shard_map/gram/pallas_call | solution.py:216
  50.7 4.5 %gram.10.kept_ref = f32[1024,512]{1,0:T(8,128)S(1)} custom-call(s32[20]{0:T(128)S(1)} %dynamic-slice_bitcast_fusion.s_ref, bf16[2048,3584]{1,0:T(8,128)(2,1)S(1)} %copy-done, bf16[512,4608]{1,0:T(8,128)(2,1)S(1)} %join.13.y_ref), custom_call_target="tpu_custom_call" | custom-call | flops 1 | bytes 1 | tf_op jit(solution)/shard_map/gram/pallas_call | solution.py:216
  60.3 7.4 %all_to_all.11 = bf16[2,128,4608]{2,1,0:T(8,128)(2,1)S(1)} all-to-all(bf16[2,128,4608]{2,1,0:T(8,128)(2,1)S(1)} %bitcast.8), channel_id=1, replica_groups={{0,8},{16,24},{32,40},{48,56},{64,72},{80,88},{96,104},{112,120},{1,9},..., dimensions={0} | all-to-all | bytes 4718592 | tf_op jit(solution)/shard_map/all_to_all | solution.py:169
  68.0 5.0 %gram.12 = s16[1024,512]{1,0:T(8,128)(2,1)S(1)} custom-call(s32[20]{0:T(128)S(1)} %dynamic-slice_bitcast_fusion.s_ref, bf16[2048,3584]{1,0:T(8,128)(2,1)S(1)} %copy-done, bf16[512,4608]{1,0:T(8,128)(2,1)S(1)} %join.17.y_ref), custom_call_target="tpu_custom_call" | custom-call | flops 1 | bytes 1 | tf_op jit(solution)/shard_map/gram/pallas_call | solution.py:216
  73.1 2.8 %collective-permute-start.15 = (s16[1024,512]{1,0:T(8,128)(2,1)S(1)}, s16[1024,512]{1,0:T(8,128)(2,1)S(1)}, u32[]{:S(2)}, u32[]{:S(2)}) collective-permute-start(s16[1024,512]{1,0:T(8,128)(2,1)S(1)} %gram.12), channel_id=1, source_target_pairs={{0,2},{1,3},{2,0},{3,1},{4,6},{5,7},{6,4},{7,5},{8,14},{9,15},{10,... | collective-permute-start | bytes 3145736 | tf_op jit(solution)/shard_map/ppermute | solution.py:70
  75.9 2.5 %gram.13 = s16[1024,512]{1,0:T(8,128)(2,1)S(1)} custom-call(s32[20]{0:T(128)S(1)} %dynamic-slice_bitcast_fusion.s_ref, bf16[2048,1024]{1,0:T(8,128)(2,1)S(1)} %copy-done.1, bf16[512,4608]{1,0:T(8,128)(2,1)S(1)} %join.17.y_ref), custom_call_target="tpu_custom_call" | custom-call | flops 1 | bytes 1 | tf_op jit(solution)/shard_map/gram/pallas_call | solution.py:216
  82.1 4.5 %gram.14.kept_ref = f32[1024,512]{1,0:T(8,128)S(1)} custom-call(s32[20]{0:T(128)S(1)} %dynamic-slice_bitcast_fusion.s_ref, bf16[2048,3584]{1,0:T(8,128)(2,1)S(1)} %copy-done, bf16[512,4608]{1,0:T(8,128)(2,1)S(1)} %join.17.y_ref), custom_call_target="tpu_custom_call" | custom-call | flops 1 | bytes 1 | tf_op jit(solution)/shard_map/gram/pallas_call | solution.py:216
  93.2 10.2 %collective-permute-done.16.in_ref = s16[1024,512]{1,0:T(8,128)(2,1)S(1)} collective-permute-done((s16[1024,512]{1,0:T(8,128)(2,1)S(1)}, s16[1024,512]{1,0:T(8,128)(2,1)S(1)}, u32[]{:S(2)}, u32[]{:S(2)}) %collective-permute-start.16) | collective-permute-done | bytes 1048608 | tf_op jit(solution)/shard_map/ppermute | solution.py:70
  110.4 6.4 %collective-permute-done.20.in_ref = s16[512,512]{1,0:T(8,128)(2,1)S(1)} collective-permute-done((s16[512,512]{1,0:T(8,128)(2,1)S(1)}, s16[512,512]{1,0:T(8,128)(2,1)S(1)}, u32[]{:S(2)}, u32[]{:S(2)}) %collective-permute-start.20) | collective-permute-done | bytes 524320 | tf_op jit(solution)/shard_map/ppermute | solution.py:70
  120.8 2.8 %collective-permute-done.24.gi_ref = s16[256,512]{1,0:T(8,128)(2,1)S(1)} collective-permute-done((s16[256,512]{1,0:T(8,128)(2,1)S(1)}, s16[256,512]{1,0:T(8,128)(2,1)S(1)}, u32[]{:S(2)}, u32[]{:S(2)}) %collective-permute-start.24) | collective-permute-done | bytes 262176 | tf_op jit(solution)/shard_map/ppermute | solution.py:70
  126.9 2.2 %collective-permute-start.25 = (f32[9,128]{1,0:T(8,128)S(1)}, f32[9,128]{1,0:T(8,128)S(1)}, u32[]{:S(2)}, u32[]{:S(2)}) collective-permute-start(f32[9,128]{1,0:T(8,128)S(1)} %pad_maximum_fusion), channel_id=1, source_target_pairs={{0,2},{1,3},{2,0},{3,1},{4,6},{5,7},{6,4},{7,5},{8,10},{9,11},{10,... | collective-permute-start | bytes 13832 | tf_op jit(solution)/shard_map/ppermute | solution.py:376
  130.1 3.7 %collective-permute-done.26 = f32[9,128]{1,0:T(8,128)S(1)} collective-permute-done((f32[9,128]{1,0:T(8,128)S(1)}, f32[9,128]{1,0:T(8,128)S(1)}, u32[]{:S(2)}, u32[]{:S(2)}) %collective-permute-start.26) | collective-permute-done | bytes 4640 | tf_op jit(solution)/shard_map/ppermute | solution.py:376
  136.5 2.4 %collective-permute-start.28 = (f32[8,128]{1,0:T(8,128)S(1)}, f32[8,128]{1,0:T(8,128)S(1)}, u32[]{:S(2)}, u32[]{:S(2)}) collective-permute-start(f32[8,128]{1,0:T(8,128)S(1)} %slice.45), channel_id=1, source_target_pairs={{0,16},{8,56},{16,0},{24,40},{32,48},{40,24},{48,32},{56,8},{64,80... | collective-permute-start | bytes 12296 | tf_op jit(solution)/shard_map/ppermute | solution.py:61
  140.1 2.5 %collective-permute-done.29 = f32[8,128]{1,0:T(8,128)S(1)} collective-permute-done((f32[8,128]{1,0:T(8,128)S(1)}, f32[8,128]{1,0:T(8,128)S(1)}, u32[]{:S(2)}, u32[]{:S(2)}) %collective-permute-start.29) | collective-permute-done | bytes 4128 | tf_op jit(solution)/shard_map/ppermute | solution.py:61
  142.6 3.5 %collective-permute-start.30 = (f32[8,128]{1,0:T(8,128)S(1)}, f32[8,128]{1,0:T(8,128)S(1)}, u32[]{:S(2)}, u32[]{:S(2)}) collective-permute-start(f32[8,128]{1,0:T(8,128)S(1)} %add.38), channel_id=1, source_target_pairs={{0,65},{1,64},{2,67},{3,66},{4,69},{5,68},{6,71},{7,70},{8,73},{9,... | collective-permute-start | bytes 12296 | tf_op jit(solution)/shard_map/ppermute | solution.py:78
  147.1 7.2 %collective-permute-start.31 = (f32[8,128]{1,0:T(8,128)S(1)}, f32[8,128]{1,0:T(8,128)S(1)}, u32[]{:S(2)}, u32[]{:S(2)}) collective-permute-start(f32[8,128]{1,0:T(8,128)S(1)} %add.39), channel_id=1, source_target_pairs={{0,8},{8,0},{16,24},{24,16},{32,40},{40,32},{48,56},{56,48},{64,72... | collective-permute-start | bytes 12296 | tf_op jit(solution)/shard_map/ppermute | solution.py:61
  (99 shorter events, 49.3 us)
Async XLA Ops:
  3.3 11.0 %collective-permute-start = (bf16[64,4608]{1,0:T(8,128)(2,1)S(1)}, bf16[64,4608]{1,0:T(8,128)(2,1)S(1)}, u32[]{:S(2)}, u32[]{:S(2)}) collective-permute-start(bf16[64,4608]{1,0:T(8,128)(2,1)S(1)} %beside.1.refs_0_), channel_id=1, source_target_pairs={{0,16},{8,56},{16,0},{24,40},{32,48},{40,24},{48,32},{56,8},{64,80... | collective-permute-start | bytes 1769480 | tf_op jit(solution)/shard_map/ppermute | solution.py:61
  6.7 17.2 %collective-permute-start.1 = (bf16[64,4608]{1,0:T(8,128)(2,1)S(1)}, bf16[64,4608]{1,0:T(8,128)(2,1)S(1)}, u32[]{:S(2)}, u32[]{:S(2)}) collective-permute-start(bf16[64,4608]{1,0:T(8,128)(2,1)S(1)} %beside.1.refs_0_), channel_id=1, source_target_pairs={{0,64},{8,72},{16,80},{24,88},{32,96},{40,104},{48,112},{56,120},{... | collective-permute-start | bytes 1769480 | tf_op jit(solution)/shard_map/ppermute | solution.py:61
  14.4 9.5 %collective-permute-start.2 = (bf16[64,4608]{1,0:T(8,128)(2,1)S(1)}, bf16[64,4608]{1,0:T(8,128)(2,1)S(1)}, u32[]{:S(2)}, u32[]{:S(2)}) collective-permute-start(bf16[64,4608]{1,0:T(8,128)(2,1)S(1)} %get-tuple-element.111), channel_id=1, source_target_pairs={{0,8},{8,0},{16,24},{24,16},{32,40},{40,32},{48,56},{56,48},{64,72... | collective-permute-start | bytes 1769480 | tf_op jit(solution)/shard_map/ppermute | solution.py:61
  14.9 9.0 %collective-permute-start.3 = (bf16[64,4608]{1,0:T(8,128)(2,1)S(1)}, bf16[64,4608]{1,0:T(8,128)(2,1)S(1)}, u32[]{:S(2)}, u32[]{:S(2)}) collective-permute-start(bf16[64,4608]{1,0:T(8,128)(2,1)S(1)} %get-tuple-element.110), channel_id=1, source_target_pairs={{0,8},{8,0},{16,24},{24,16},{32,40},{40,32},{48,56},{56,48},{64,72... | collective-permute-start | bytes 1769480 | tf_op jit(solution)/shard_map/ppermute | solution.py:61
  15.0 9.1 %collective-permute-start.4 = (bf16[64,4608]{1,0:T(8,128)(2,1)S(1)}, bf16[64,4608]{1,0:T(8,128)(2,1)S(1)}, u32[]{:S(2)}, u32[]{:S(2)}) collective-permute-start(bf16[64,4608]{1,0:T(8,128)(2,1)S(1)} %get-tuple-element.111), channel_id=1, source_target_pairs={{0,48},{8,24},{16,32},{24,8},{32,16},{40,56},{48,0},{56,40},{64,11... | collective-permute-start | bytes 1769480 | tf_op jit(solution)/shard_map/ppermute | solution.py:61
  16.3 14.1 %collective-permute-start.5 = (bf16[64,4608]{1,0:T(8,128)(2,1)S(1)}, bf16[64,4608]{1,0:T(8,128)(2,1)S(1)}, u32[]{:S(2)}, u32[]{:S(2)}) collective-permute-start(bf16[64,4608]{1,0:T(8,128)(2,1)S(1)} %get-tuple-element.110), channel_id=1, source_target_pairs={{0,48},{8,24},{16,32},{24,8},{32,16},{40,56},{48,0},{56,40},{64,11... | collective-permute-start | bytes 1769480 | tf_op jit(solution)/shard_map/ppermute | solution.py:61
  30.5 11.1 %collective-permute-start.10 = (bf16[64,4608]{1,0:T(8,128)(2,1)S(1)}, bf16[64,4608]{1,0:T(8,128)(2,1)S(1)}, u32[]{:S(2)}, u32[]{:S(2)}) collective-permute-start(bf16[64,4608]{1,0:T(8,128)(2,1)S(1)} %join.10.refs_0_), channel_id=1, source_target_pairs={{0,16},{8,56},{16,0},{24,40},{32,48},{40,24},{48,32},{56,8},{64,80... | collective-permute-start | bytes 1769480 | tf_op jit(solution)/shard_map/ppermute | solution.py:61
  41.7 8.9 %collective-permute-start.11 = (bf16[128,4608]{1,0:T(8,128)(2,1)S(1)}, bf16[128,4608]{1,0:T(8,128)(2,1)S(1)}, u32[]{:S(2)}, u32[]{:S(2)}) collective-permute-start(bf16[128,4608]{1,0:T(8,128)(2,1)S(1)} %join.14.refs_0_), channel_id=1, source_target_pairs={{0,8},{8,0},{16,24},{24,16},{32,40},{40,32},{48,56},{56,48},{64,72... | collective-permute-start | bytes 3538952 | tf_op jit(solution)/shard_map/ppermute | solution.py:61
  43.1 15.3 %collective-permute-start.12 = (bf16[128,4608]{1,0:T(8,128)(2,1)S(1)}, bf16[128,4608]{1,0:T(8,128)(2,1)S(1)}, u32[]{:S(2)}, u32[]{:S(2)}) collective-permute-start(bf16[128,4608]{1,0:T(8,128)(2,1)S(1)} %join.14.refs_0_), channel_id=1, source_target_pairs={{0,48},{8,24},{16,32},{24,8},{32,16},{40,56},{48,0},{56,40},{64,11... | collective-permute-start | bytes 3538952 | tf_op jit(solution)/shard_map/ppermute | solution.py:61
  43.3 15.3 %collective-permute-start.13 = (s16[1024,512]{1,0:T(8,128)(2,1)S(1)}, s16[1024,512]{1,0:T(8,128)(2,1)S(1)}, u32[]{:S(2)}, u32[]{:S(2)}) collective-permute-start(s16[1024,512]{1,0:T(8,128)(2,1)S(1)} %gram.8), channel_id=1, source_target_pairs={{0,2},{1,3},{2,0},{3,1},{4,6},{5,7},{6,4},{7,5},{8,14},{9,15},{10,... | collective-permute-start | bytes 3145736 | tf_op jit(solution)/shard_map/ppermute | solution.py:70
  48.7 31.5 %collective-permute-start.14 = (s16[1024,512]{1,0:T(8,128)(2,1)S(1)}, s16[1024,512]{1,0:T(8,128)(2,1)S(1)}, u32[]{:S(2)}, u32[]{:S(2)}) collective-permute-start(s16[1024,512]{1,0:T(8,128)(2,1)S(1)} %gram.9), channel_id=1, source_target_pairs={{0,1},{1,0},{2,3},{3,2},{4,5},{5,4},{6,7},{7,6},{8,9},{9,8},{10,11... | collective-permute-start | bytes 3145736 | tf_op jit(solution)/shard_map/ppermute | solution.py:70
  73.1 17.7 %collective-permute-start.15 = (s16[1024,512]{1,0:T(8,128)(2,1)S(1)}, s16[1024,512]{1,0:T(8,128)(2,1)S(1)}, u32[]{:S(2)}, u32[]{:S(2)}) collective-permute-start(s16[1024,512]{1,0:T(8,128)(2,1)S(1)} %gram.12), channel_id=1, source_target_pairs={{0,2},{1,3},{2,0},{3,1},{4,6},{5,7},{6,4},{7,5},{8,14},{9,15},{10,... | collective-permute-start | bytes 3145736 | tf_op jit(solution)/shard_map/ppermute | solution.py:70
  78.4 24.9 %collective-permute-start.16 = (s16[1024,512]{1,0:T(8,128)(2,1)S(1)}, s16[1024,512]{1,0:T(8,128)(2,1)S(1)}, u32[]{:S(2)}, u32[]{:S(2)}) collective-permute-start(s16[1024,512]{1,0:T(8,128)(2,1)S(1)} %gram.13), channel_id=1, source_target_pairs={{0,1},{1,0},{2,3},{3,2},{4,5},{5,4},{6,7},{7,6},{8,9},{9,8},{10,11... | collective-permute-start | bytes 3145736 | tf_op jit(solution)/shard_map/ppermute | solution.py:70
  81.8 23.3 %collective-permute-start.17 = (s16[512,512]{1,0:T(8,128)(2,1)S(1)}, s16[512,512]{1,0:T(8,128)(2,1)S(1)}, u32[]{:S(2)}, u32[]{:S(2)}) collective-permute-start(s16[512,512]{1,0:T(8,128)(2,1)S(1)} %get-tuple-element.85), channel_id=1, source_target_pairs={{0,6},{1,7},{2,4},{3,5},{4,2},{5,3},{6,0},{7,1},{8,10},{9,11},{10,... | collective-permute-start | bytes 1572872 | tf_op jit(solution)/shard_map/ppermute | solution.py:70
  86.7 19.6 %collective-permute-start.18 = (s16[512,512]{1,0:T(8,128)(2,1)S(1)}, s16[512,512]{1,0:T(8,128)(2,1)S(1)}, u32[]{:S(2)}, u32[]{:S(2)}) collective-permute-start(s16[512,512]{1,0:T(8,128)(2,1)S(1)} %get-tuple-element.88), channel_id=1, source_target_pairs={{0,2},{1,3},{2,0},{3,1},{4,6},{5,7},{6,4},{7,5},{8,14},{9,15},{10,... | collective-permute-start | bytes 1572872 | tf_op jit(solution)/shard_map/ppermute | solution.py:70
  92.4 16.9 %collective-permute-start.19 = (s16[512,512]{1,0:T(8,128)(2,1)S(1)}, s16[512,512]{1,0:T(8,128)(2,1)S(1)}, u32[]{:S(2)}, u32[]{:S(2)}) collective-permute-start(s16[512,512]{1,0:T(8,128)(2,1)S(1)} %get-tuple-element.91), channel_id=1, source_target_pairs={{0,6},{1,7},{2,4},{3,5},{4,2},{5,3},{6,0},{7,1},{8,10},{9,11},{10,... | collective-permute-start | bytes 1572872 | tf_op jit(solution)/shard_map/ppermute | solution.py:70
  105.0 11.8 %collective-permute-start.20 = (s16[512,512]{1,0:T(8,128)(2,1)S(1)}, s16[512,512]{1,0:T(8,128)(2,1)S(1)}, u32[]{:S(2)}, u32[]{:S(2)}) collective-permute-start(s16[512,512]{1,0:T(8,128)(2,1)S(1)} %get-tuple-element.94), channel_id=1, source_target_pairs={{0,2},{1,3},{2,0},{3,1},{4,6},{5,7},{6,4},{7,5},{8,14},{9,15},{10,... | collective-permute-start | bytes 1572872 | tf_op jit(solution)/shard_map/ppermute | solution.py:70
  107.4 12.2 %collective-permute-start.22 = (s16[256,512]{1,0:T(8,128)(2,1)S(1)}, s16[256,512]{1,0:T(8,128)(2,1)S(1)}, u32[]{:S(2)}, u32[]{:S(2)}) collective-permute-start(s16[256,512]{1,0:T(8,128)(2,1)S(1)} %get-tuple-element.98), channel_id=1, source_target_pairs={{0,6},{1,7},{2,4},{3,5},{4,2},{5,3},{6,0},{7,1},{8,10},{9,11},{10,... | collective-permute-start | bytes 786440 | tf_op jit(solution)/shard_map/ppermute | solution.py:70
  107.6 12.0 %collective-permute-start.21 = (s16[256,512]{1,0:T(8,128)(2,1)S(1)}, s16[256,512]{1,0:T(8,128)(2,1)S(1)}, u32[]{:S(2)}, u32[]{:S(2)}) collective-permute-start(s16[256,512]{1,0:T(8,128)(2,1)S(1)} %get-tuple-element.97), channel_id=1, source_target_pairs={{0,1},{1,0},{2,3},{3,2},{4,5},{5,4},{6,7},{7,6},{8,9},{9,8},{10,11... | collective-permute-start | bytes 786440 | tf_op jit(solution)/shard_map/ppermute | solution.py:70
  117.9 5.6 %collective-permute-start.24 = (s16[256,512]{1,0:T(8,128)(2,1)S(1)}, s16[256,512]{1,0:T(8,128)(2,1)S(1)}, u32[]{:S(2)}, u32[]{:S(2)}) collective-permute-start(s16[256,512]{1,0:T(8,128)(2,1)S(1)} %get-tuple-element.102), channel_id=1, source_target_pairs={{0,6},{1,7},{2,4},{3,5},{4,2},{5,3},{6,0},{7,1},{8,10},{9,11},{10,... | collective-permute-start | bytes 786440 | tf_op jit(solution)/shard_map/ppermute | solution.py:70
  118.0 7.5 %collective-permute-start.23 = (s16[256,512]{1,0:T(8,128)(2,1)S(1)}, s16[256,512]{1,0:T(8,128)(2,1)S(1)}, u32[]{:S(2)}, u32[]{:S(2)}) collective-permute-start(s16[256,512]{1,0:T(8,128)(2,1)S(1)} %get-tuple-element.101), channel_id=1, source_target_pairs={{0,1},{1,0},{2,3},{3,2},{4,5},{5,4},{6,7},{7,6},{8,9},{9,8},{10,11... | collective-permute-start | bytes 786440 | tf_op jit(solution)/shard_map/ppermute | solution.py:70
  130.1 3.7 %collective-permute-start.26 = (f32[9,128]{1,0:T(8,128)S(1)}, f32[9,128]{1,0:T(8,128)S(1)}, u32[]{:S(2)}, u32[]{:S(2)}) collective-permute-start(f32[9,128]{1,0:T(8,128)S(1)} %fusion.2), channel_id=1, source_target_pairs={{0,6},{1,7},{2,4},{3,5},{4,2},{5,3},{6,0},{7,1},{8,14},{9,15},{10,... | collective-permute-start | bytes 13832 | tf_op jit(solution)/shard_map/ppermute | solution.py:376
  142.6 4.5 %collective-permute-start.30 = (f32[8,128]{1,0:T(8,128)S(1)}, f32[8,128]{1,0:T(8,128)S(1)}, u32[]{:S(2)}, u32[]{:S(2)}) collective-permute-start(f32[8,128]{1,0:T(8,128)S(1)} %add.38), channel_id=1, source_target_pairs={{0,65},{1,64},{2,67},{3,66},{4,69},{5,68},{6,71},{7,70},{8,73},{9,... | collective-permute-start | bytes 12296 | tf_op jit(solution)/shard_map/ppermute | solution.py:78
  147.1 8.0 %collective-permute-start.31 = (f32[8,128]{1,0:T(8,128)S(1)}, f32[8,128]{1,0:T(8,128)S(1)}, u32[]{:S(2)}, u32[]{:S(2)}) collective-permute-start(f32[8,128]{1,0:T(8,128)S(1)} %add.39), channel_id=1, source_target_pairs={{0,8},{8,0},{16,24},{24,16},{32,40},{40,32},{48,56},{56,48},{64,72... | collective-permute-start | bytes 12296 | tf_op jit(solution)/shard_map/ppermute | solution.py:61
  (13 other events, 56.9 us)
where the time goes:
time: 156 us
  waiting for transfers between devices  54.6 us (35%)
  starting transfers between devices  45.9 us (29%)
  Pallas kernels  42.5 us (27%)
  blocking collectives  7.44 us (5%)
  local copies, waits for them, and re-layouts  3.01 us (2%)
    pallas_call x8, Pallas kernels, gram(): pl.pallas_call(kernel, out_shape=pltpu.VMEM((rows, n), jnp.int16 if away...  27.8 us
    ppermute x16, waiting for transfers between devices, send_dp(): return lax.ppermute(x, 'dp', [(d, fn(d)) for d in range(DP)])  24.8 us
    ppermute x16, starting transfers between devices, send_dp(): return lax.ppermute(x, 'dp', [(d, fn(d)) for d in range(DP)])  24.2 us
    ppermute x12, waiting for transfers between devices, send_link(): return lax.ppermute(x, ('dp', 'tensor'), pairs)  23 us
    ppermute x12, starting transfers between devices, send_link(): return lax.ppermute(x, ('dp', 'tensor'), pairs)  14.6 us
    pallas_call x8, Pallas kernels, fold(): pl.pallas_call(kernel, out_shape=(pltpu.VMEM((half, n), jnp.int16), pltpu...  11.1 us
    all_to_all x1, blocking collectives, both_cores(): lax.all_to_all(twice, 'dp', 0, 0, axis_index_groups=groups, tiled=True)  7.44 us
    ppermute x3, waiting for transfers between devices, local(): lax.ppermute(total, 'tensor', [(i, along_link(i, link)) for i in range(TE...  5.87 us
  transfers between devices with their start and end apart: 32, of which 20 were waited for; matrix products, arithmetic and copies ran while one was open for 0% of the time, Pallas kernels for 26%

commit v1 on v0

--- a/solution.py
+++ b/solution.py
@@ -101,6 +101,7 @@
 
 IN_VMEM = pl.BlockSpec(memory_space=pltpu.VMEM)
 IN_SMEM = pl.BlockSpec(memory_space=pltpu.SMEM)
+IN_HBM = pl.BlockSpec(memory_space=pltpu.HBM)
 BRIEF = pl.CostEstimate(flops=1, bytes_accessed=1, transcendentals=0)
 
 
@@ -140,19 +141,26 @@
 
 
 def beside(hidden, grad):
-    def kernel(hidden_ref, grad_ref, out_ref):
-        out_ref[:, :HIDDEN_DEV] = hidden_ref[...]
-        out_ref[:, HIDDEN_DEV:] = grad_ref[...]
+    def kernel(hidden_ref, grad_ref, out_ref, sem):
+        copies = [
+            pltpu.make_async_copy(hidden_ref, out_ref.at[:, :HIDDEN_DEV], sem.at[0]),
+            pltpu.make_async_copy(grad_ref, out_ref.at[:, HIDDEN_DEV:], sem.at[1]),
+        ]
+        for copy in copies:
+            copy.start()
+        for copy in copies:
+            copy.wait()
 
     return pl.pallas_call(
         kernel,
         out_shape=pltpu.VMEM((VAL_DEV, HIDDEN_DEV + GRAD_DEV), hidden.dtype),
-        in_specs=[IN_VMEM, IN_VMEM],
+        in_specs=[IN_HBM, IN_HBM],
         out_specs=IN_VMEM,
-        compiler_params=params(4),
+        scratch_shapes=[pltpu.SemaphoreType.DMA((2,))],
+        compiler_params=params(1),
         cost_estimate=BRIEF,
         name="beside",
-    )(vmem(hidden), vmem(grad))
+    )(*[pltpu.with_memory_space_constraint(a, pltpu.HBM) for a in (hidden, grad)])
 
 
 def tie(x, after):
@@ -225,17 +233,20 @@
     )(scalars, vmem(x), vmem(y))
 
 
-def fold(scalars, kept, arrived, bit):
+def fold(scalars, kept, arrived, bit, run=None):
     rows, n = kept.shape
     half = rows // 2
+    run = run or half
 
     def kernel(s_ref, kept_ref, in_ref, send_ref, out_ref):
         keep = s_ref[bit]
 
         @pl.loop(0, half // GROUP)
         def _(r):
-            away = part((1 - keep) * half + r * GROUP, GROUP)
-            stay = part(keep * half + r * GROUP, GROUP)
+            row = r * GROUP
+            base = row // run * 2 * run + row % run
+            away = part(base + (1 - keep) * run, GROUP)
+            stay = part(base + keep * run, GROUP)
             to = part(r * GROUP, GROUP)
             for c in range(0, n, 128):
                 c = slice(c, c + 128)
@@ -324,8 +335,8 @@
     def keep_half(x, vals, bit):
         return ordered(gram(scalars, x, after(vals), bit, False))
 
-    def folded(kept, arrived, bit):
-        send, kept = fold(scalars, after(kept), arrived, bit)
+    def folded(kept, arrived, bit, run=None):
+        send, kept = fold(scalars, after(kept), arrived, bit, run)
         ordered(kept)
         return kept, send_link(send, bit)
 
@@ -338,7 +349,7 @@
     far0 = joined(far0)
     near_half = joined(near_pair, *near_c1)
     near2 = joined(*near2)
-    near_c2 = pieces(near2, 4, along_core)
+    near_c2 = pieces(near2, 1, along_core)
     far1 = send_dp(after(far0), first_x)
     near = joined(near_half, near2, *near_c2)
 
@@ -353,17 +364,18 @@
     far_rest = both_cores(joined(far2, far2))
     act0, act0_in = folded(act0, act0_in, 1)
     far = joined(far_half, far_rest)
+    grad1_in = send_half(train_grad, far, 2)
     act1_in = send_half(train_hidden, far, 0)
-    grad1_in = send_half(train_grad, far, 2)
     grad0, grad0_in = folded(grad0, grad0_in, 0)
     act1 = keep_half(train_hidden, far, 0)
     grad1 = keep_half(train_grad, far, 2)
-    act1, act1_in = folded(act1, act1_in, 1)
     grad1, grad1_in = folded(grad1, grad1_in, 0)
+    act1, act1_in = folded(act1, act1_in, 2, LEAF)
     act0, act0_in = folded(act0, act0_in, 2)
     grad0, grad0_in = folded(grad0, grad0_in, 1)
-    act1, act1_in = folded(act1, act1_in, 2)
     grad1, grad1_in = folded(grad1, grad1_in, 1)
+    act1, act1_in = folded(act1, act1_in, 1)
+    last[0] = (last[0], grad1_in)
     col0, seq0 = finish(scalars, after(act0), act0_in, grad0, grad0_in, seq_ids)
     ordered(col0)
     col1, seq1 = finish(scalars, after(act1), act1_in, grad1, grad1_in, seq_ids)

time: 156 us -> 154 us (0.987)
  waiting for transfers between devices: 54.6 us -> 49.8 us
  starting transfers between devices: 45.9 us -> 49.1 us
  local copies, waits for them, and re-layouts: 3.01 us -> 1.01 us
    ppermute x12, waiting for transfers between devices: 23 us -> 18.3 us  [send_link(): return lax.ppermute(x, ('dp', 'tensor'), pairs)]
    ppermute x16 -> x13, starting transfers between devices: 24.2 us -> 26.6 us  [send_dp(): return lax.ppermute(x, 'dp', [(d, fn(d)) for d in range(DP)])]
    unnamed x10 -> x6, local copies, waits for them, and re-layouts: 1.94 us -> 0.02 us
    ppermute x16 -> x13, waiting for transfers between devices: 24.8 us -> 25.1 us  [send_dp(): return lax.ppermute(x, 'dp', [(d, fn(d)) for d in range(DP)])]
  transfers between devices with their start and end apart: 32 -> 29, of which waited for: 20 -> 18; matrix products, arithmetic and copies ran while one was open for 0% -> 0% of each run, Pallas kernels for 26% -> 27%
where the time goes in v1:
time: 154 us
  waiting for transfers between devices  49.8 us (32%)
  starting transfers between devices  49.1 us (32%)
  Pallas kernels  43.8 us (28%)
  blocking collectives  7.8 us (5%)
    pallas_call x8, Pallas kernels, gram(): pl.pallas_call(kernel, out_shape=pltpu.VMEM((rows, n), jnp.int16 if away...  27.7 us
    ppermute x13, starting transfers between devices, send_dp(): return lax.ppermute(x, 'dp', [(d, fn(d)) for d in range(DP)])  26.6 us
    ppermute x13, waiting for transfers between devices, send_dp(): return lax.ppermute(x, 'dp', [(d, fn(d)) for d in range(DP)])  25.1 us
    ppermute x12, waiting for transfers between devices, send_link(): return lax.ppermute(x, ('dp', 'tensor'), pairs)  18.3 us
    ppermute x12, starting transfers between devices, send_link(): return lax.ppermute(x, ('dp', 'tensor'), pairs)  15.7 us
    pallas_call x8, Pallas kernels, fold(): pl.pallas_call(kernel, out_shape=(pltpu.VMEM((half, n), jnp.int16), pltpu...  11.3 us
    all_to_all x1, blocking collectives, both_cores(): lax.all_to_all(twice, 'dp', 0, 0, axis_index_groups=groups, tiled=True)  7.8 us
    ppermute x3, waiting for transfers between devices, local(): lax.ppermute(total, 'tensor', [(i, along_link(i, link)) for i in range(TE...  5.4 us
  transfers between devices with their start and end apart: 29, of which 18 were waited for; matrix products, arithmetic and copies ran while one was open for 0% of the time, Pallas kernels for 27%

profile of v1, /device:TPU:1, one launch (start us, length us, event | category | flops | bytes accessed | tf_op | source)
XLA Modules:
  0.0 153.7 jit_solution(1214867956353596274)
XLA Ops:
  2.4 3.4 %collective-permute-start = (bf16[64,4608]{1,0:T(8,128)(2,1)S(1)}, bf16[64,4608]{1,0:T(8,128)(2,1)S(1)}, u32[]{:S(2)}, u32[]{:S(2)}) collective-permute-start(bf16[64,4608]{1,0:T(8,128)(2,1)S(1)} %beside.1.refs_0_), channel_id=1, source_target_pairs={{0,16},{8,56},{16,0},{24,40},{32,48},{40,24},{48,32},{56,8},{64,80... | collective-permute-start | bytes 1769480 | tf_op jit(solution)/shard_map/ppermute | solution.py:61
  5.8 3.6 %collective-permute-start.1 = (bf16[64,4608]{1,0:T(8,128)(2,1)S(1)}, bf16[64,4608]{1,0:T(8,128)(2,1)S(1)}, u32[]{:S(2)}, u32[]{:S(2)}) collective-permute-start(bf16[64,4608]{1,0:T(8,128)(2,1)S(1)} %beside.1.refs_0_), channel_id=1, source_target_pairs={{0,64},{8,72},{16,80},{24,88},{32,96},{40,104},{48,112},{56,120},{... | collective-permute-start | bytes 1769480 | tf_op jit(solution)/shard_map/ppermute | solution.py:61
  9.4 4.0 %collective-permute-done.refs_1_ = bf16[64,4608]{1,0:T(8,128)(2,1)S(1)} collective-permute-done((bf16[64,4608]{1,0:T(8,128)(2,1)S(1)}, bf16[64,4608]{1,0:T(8,128)(2,1)S(1)}, u32[]{:S(2)}, u32[]{:S(2)}) %collective-permute-start) | collective-permute-done | bytes 589856 | tf_op jit(solution)/shard_map/ppermute | solution.py:61
  15.6 7.4 %collective-permute-done.1.refs_0_ = bf16[64,4608]{1,0:T(8,128)(2,1)S(1)} collective-permute-done((bf16[64,4608]{1,0:T(8,128)(2,1)S(1)}, bf16[64,4608]{1,0:T(8,128)(2,1)S(1)}, u32[]{:S(2)}, u32[]{:S(2)}) %collective-permute-start.1) | collective-permute-done | bytes 589856 | tf_op jit(solution)/shard_map/ppermute | solution.py:61
  23.2 6.2 %collective-permute-done.5.refs_1_ = bf16[64,4608]{1,0:T(8,128)(2,1)S(1)} collective-permute-done((bf16[64,4608]{1,0:T(8,128)(2,1)S(1)}, bf16[64,4608]{1,0:T(8,128)(2,1)S(1)}, u32[]{:S(2)}, u32[]{:S(2)}) %collective-permute-start.5) | collective-permute-done | bytes 589856 | tf_op jit(solution)/shard_map/ppermute | solution.py:61
  29.6 2.6 %collective-permute-start.6 = (bf16[128,4608]{1,0:T(8,128)(2,1)S(1)}, bf16[128,4608]{1,0:T(8,128)(2,1)S(1)}, u32[]{:S(2)}, u32[]{:S(2)}) collective-permute-start(bf16[128,4608]{1,0:T(8,128)(2,1)S(1)} %join.12.refs_1_), channel_id=1, source_target_pairs={{0,8},{8,0},{16,24},{24,16},{32,40},{40,32},{48,56},{56,48},{64,72... | collective-permute-start | bytes 3538952 | tf_op jit(solution)/shard_map/ppermute | solution.py:61
  32.1 2.6 %collective-permute-start.7 = (bf16[64,4608]{1,0:T(8,128)(2,1)S(1)}, bf16[64,4608]{1,0:T(8,128)(2,1)S(1)}, u32[]{:S(2)}, u32[]{:S(2)}) collective-permute-start(bf16[64,4608]{1,0:T(8,128)(2,1)S(1)} %join.10.refs_0_), channel_id=1, source_target_pairs={{0,16},{8,56},{16,0},{24,40},{32,48},{40,24},{48,32},{56,8},{64,80... | collective-permute-start | bytes 1769480 | tf_op jit(solution)/shard_map/ppermute | solution.py:61
  35.0 5.0 %gram.8 = s16[1024,512]{1,0:T(8,128)(2,1)S(1)} custom-call(s32[20]{0:T(128)S(1)} %dynamic-slice_bitcast_fusion.s_ref, bf16[2048,3584]{1,0:T(8,128)(2,1)S(1)} %copy-done, bf16[512,4608]{1,0:T(8,128)(2,1)S(1)} %join.13.y_ref), custom_call_target="tpu_custom_call" | custom-call | flops 1 | bytes 1 | tf_op jit(solution)/shard_map/gram/pallas_call | solution.py:224
  42.3 2.9 %collective-permute-start.10 = (s16[1024,512]{1,0:T(8,128)(2,1)S(1)}, s16[1024,512]{1,0:T(8,128)(2,1)S(1)}, u32[]{:S(2)}, u32[]{:S(2)}) collective-permute-start(s16[1024,512]{1,0:T(8,128)(2,1)S(1)} %gram.8), channel_id=1, source_target_pairs={{0,2},{1,3},{2,0},{3,1},{4,6},{5,7},{6,4},{7,5},{8,14},{9,15},{10,... | collective-permute-start | bytes 3145736 | tf_op jit(solution)/shard_map/ppermute | solution.py:70
  45.2 2.5 %gram.9 = s16[1024,512]{1,0:T(8,128)(2,1)S(1)} custom-call(s32[20]{0:T(128)S(1)} %dynamic-slice_bitcast_fusion.s_ref, bf16[2048,1024]{1,0:T(8,128)(2,1)S(1)} %copy-done.1, bf16[512,4608]{1,0:T(8,128)(2,1)S(1)} %join.13.y_ref), custom_call_target="tpu_custom_call" | custom-call | flops 1 | bytes 1 | tf_op jit(solution)/shard_map/gram/pallas_call | solution.py:224
  49.8 4.5 %gram.10.kept_ref = f32[1024,512]{1,0:T(8,128)S(1)} custom-call(s32[20]{0:T(128)S(1)} %dynamic-slice_bitcast_fusion.s_ref, bf16[2048,3584]{1,0:T(8,128)(2,1)S(1)} %copy-done, bf16[512,4608]{1,0:T(8,128)(2,1)S(1)} %join.13.y_ref), custom_call_target="tpu_custom_call" | custom-call | flops 1 | bytes 1 | tf_op jit(solution)/shard_map/gram/pallas_call | solution.py:224
  59.5 7.8 %all_to_all.11 = bf16[2,128,4608]{2,1,0:T(8,128)(2,1)S(1)} all-to-all(bf16[2,128,4608]{2,1,0:T(8,128)(2,1)S(1)} %bitcast.8), channel_id=1, replica_groups={{0,8},{16,24},{32,40},{48,56},{64,72},{80,88},{96,104},{112,120},{1,9},..., dimensions={0} | all-to-all | bytes 4718592 | tf_op jit(solution)/shard_map/all_to_all | solution.py:177
  67.6 2.5 %gram.12 = s16[1024,512]{1,0:T(8,128)(2,1)S(1)} custom-call(s32[20]{0:T(128)S(1)} %dynamic-slice_bitcast_fusion.s_ref, bf16[2048,1024]{1,0:T(8,128)(2,1)S(1)} %copy-done.1, bf16[512,4608]{1,0:T(8,128)(2,1)S(1)} %join.17.y_ref), custom_call_target="tpu_custom_call" | custom-call | flops 1 | bytes 1 | tf_op jit(solution)/shard_map/gram/pallas_call | solution.py:224
  71.9 5.0 %gram.13 = s16[1024,512]{1,0:T(8,128)(2,1)S(1)} custom-call(s32[20]{0:T(128)S(1)} %dynamic-slice_bitcast_fusion.s_ref, bf16[2048,3584]{1,0:T(8,128)(2,1)S(1)} %copy-done, bf16[512,4608]{1,0:T(8,128)(2,1)S(1)} %join.17.y_ref), custom_call_target="tpu_custom_call" | custom-call | flops 1 | bytes 1 | tf_op jit(solution)/shard_map/gram/pallas_call | solution.py:224
  77.0 2.8 %collective-permute-start.13 = (s16[1024,512]{1,0:T(8,128)(2,1)S(1)}, s16[1024,512]{1,0:T(8,128)(2,1)S(1)}, u32[]{:S(2)}, u32[]{:S(2)}) collective-permute-start(s16[1024,512]{1,0:T(8,128)(2,1)S(1)} %gram.13), channel_id=1, source_target_pairs={{0,2},{1,3},{2,0},{3,1},{4,6},{5,7},{6,4},{7,5},{8,14},{9,15},{10,... | collective-permute-start | bytes 3145736 | tf_op jit(solution)/shard_map/ppermute | solution.py:70
  81.8 4.5 %gram.14.kept_ref = f32[1024,512]{1,0:T(8,128)S(1)} custom-call(s32[20]{0:T(128)S(1)} %dynamic-slice_bitcast_fusion.s_ref, bf16[2048,3584]{1,0:T(8,128)(2,1)S(1)} %copy-done, bf16[512,4608]{1,0:T(8,128)(2,1)S(1)} %join.17.y_ref), custom_call_target="tpu_custom_call" | custom-call | flops 1 | bytes 1 | tf_op jit(solution)/shard_map/gram/pallas_call | solution.py:224
  88.8 6.6 %collective-permute-done.12.in_ref = s16[1024,512]{1,0:T(8,128)(2,1)S(1)} collective-permute-done((s16[1024,512]{1,0:T(8,128)(2,1)S(1)}, s16[1024,512]{1,0:T(8,128)(2,1)S(1)}, u32[]{:S(2)}, u32[]{:S(2)}) %collective-permute-start.12) | collective-permute-done | bytes 1048608 | tf_op jit(solution)/shard_map/ppermute | solution.py:70
  104.9 3.9 %collective-permute-done.16.in_ref = s16[512,512]{1,0:T(8,128)(2,1)S(1)} collective-permute-done((s16[512,512]{1,0:T(8,128)(2,1)S(1)}, s16[512,512]{1,0:T(8,128)(2,1)S(1)}, u32[]{:S(2)}, u32[]{:S(2)}) %collective-permute-start.16) | collective-permute-done | bytes 524320 | tf_op jit(solution)/shard_map/ppermute | solution.py:70
  111.5 3.5 %collective-permute-done.17.in_ref = s16[512,512]{1,0:T(8,128)(2,1)S(1)} collective-permute-done((s16[512,512]{1,0:T(8,128)(2,1)S(1)}, s16[512,512]{1,0:T(8,128)(2,1)S(1)}, u32[]{:S(2)}, u32[]{:S(2)}) %collective-permute-start.17) | collective-permute-done | bytes 524320 | tf_op jit(solution)/shard_map/ppermute | solution.py:70
  123.2 2.5 %collective-permute-done.22 = f32[9,128]{1,0:T(8,128)S(1)} collective-permute-done((f32[9,128]{1,0:T(8,128)S(1)}, f32[9,128]{1,0:T(8,128)S(1)}, u32[]{:S(2)}, u32[]{:S(2)}) %collective-permute-start.22) | collective-permute-done | bytes 4640 | tf_op jit(solution)/shard_map/ppermute | solution.py:388
  131.9 2.5 %collective-permute-start.25 = (f32[8,128]{1,0:T(8,128)S(1)}, f32[8,128]{1,0:T(8,128)S(1)}, u32[]{:S(2)}, u32[]{:S(2)}) collective-permute-start(f32[8,128]{1,0:T(8,128)S(1)} %slice.25), channel_id=1, source_target_pairs={{0,16},{8,56},{16,0},{24,40},{32,48},{40,24},{48,32},{56,8},{64,80... | collective-permute-start | bytes 12296 | tf_op jit(solution)/shard_map/ppermute | solution.py:61
  135.6 2.5 %collective-permute-done.26 = f32[8,128]{1,0:T(8,128)S(1)} collective-permute-done((f32[8,128]{1,0:T(8,128)S(1)}, f32[8,128]{1,0:T(8,128)S(1)}, u32[]{:S(2)}, u32[]{:S(2)}) %collective-permute-start.26) | collective-permute-done | bytes 4128 | tf_op jit(solution)/shard_map/ppermute | solution.py:61
  138.1 3.4 %collective-permute-start.27 = (f32[8,128]{1,0:T(8,128)S(1)}, f32[8,128]{1,0:T(8,128)S(1)}, u32[]{:S(2)}, u32[]{:S(2)}) collective-permute-start(f32[8,128]{1,0:T(8,128)S(1)} %add.38), channel_id=1, source_target_pairs={{0,65},{1,64},{2,67},{3,66},{4,69},{5,68},{6,71},{7,70},{8,73},{9,... | collective-permute-start | bytes 12296 | tf_op jit(solution)/shard_map/ppermute | solution.py:78
  142.5 9.8 %collective-permute-start.28 = (f32[8,128]{1,0:T(8,128)S(1)}, f32[8,128]{1,0:T(8,128)S(1)}, u32[]{:S(2)}, u32[]{:S(2)}) collective-permute-start(f32[8,128]{1,0:T(8,128)S(1)} %add.39), channel_id=1, source_target_pairs={{0,8},{8,0},{16,24},{24,16},{32,40},{40,32},{48,56},{56,48},{64,72... | collective-permute-start | bytes 12296 | tf_op jit(solution)/shard_map/ppermute | solution.py:61
  (88 shorter events, 50.8 us)
Async XLA Ops:
  2.4 11.0 %collective-permute-start = (bf16[64,4608]{1,0:T(8,128)(2,1)S(1)}, bf16[64,4608]{1,0:T(8,128)(2,1)S(1)}, u32[]{:S(2)}, u32[]{:S(2)}) collective-permute-start(bf16[64,4608]{1,0:T(8,128)(2,1)S(1)} %beside.1.refs_0_), channel_id=1, source_target_pairs={{0,16},{8,56},{16,0},{24,40},{32,48},{40,24},{48,32},{56,8},{64,80... | collective-permute-start | bytes 1769480 | tf_op jit(solution)/shard_map/ppermute | solution.py:61
  5.8 17.2 %collective-permute-start.1 = (bf16[64,4608]{1,0:T(8,128)(2,1)S(1)}, bf16[64,4608]{1,0:T(8,128)(2,1)S(1)}, u32[]{:S(2)}, u32[]{:S(2)}) collective-permute-start(bf16[64,4608]{1,0:T(8,128)(2,1)S(1)} %beside.1.refs_0_), channel_id=1, source_target_pairs={{0,64},{8,72},{16,80},{24,88},{32,96},{40,104},{48,112},{56,120},{... | collective-permute-start | bytes 1769480 | tf_op jit(solution)/shard_map/ppermute | solution.py:61
  13.5 9.5 %collective-permute-start.2 = (bf16[64,4608]{1,0:T(8,128)(2,1)S(1)}, bf16[64,4608]{1,0:T(8,128)(2,1)S(1)}, u32[]{:S(2)}, u32[]{:S(2)}) collective-permute-start(bf16[64,4608]{1,0:T(8,128)(2,1)S(1)} %get-tuple-element.105), channel_id=1, source_target_pairs={{0,8},{8,0},{16,24},{24,16},{32,40},{40,32},{48,56},{56,48},{64,72... | collective-permute-start | bytes 1769480 | tf_op jit(solution)/shard_map/ppermute | solution.py:61
  14.0 9.0 %collective-permute-start.3 = (bf16[64,4608]{1,0:T(8,128)(2,1)S(1)}, bf16[64,4608]{1,0:T(8,128)(2,1)S(1)}, u32[]{:S(2)}, u32[]{:S(2)}) collective-permute-start(bf16[64,4608]{1,0:T(8,128)(2,1)S(1)} %get-tuple-element.104), channel_id=1, source_target_pairs={{0,8},{8,0},{16,24},{24,16},{32,40},{40,32},{48,56},{56,48},{64,72... | collective-permute-start | bytes 1769480 | tf_op jit(solution)/shard_map/ppermute | solution.py:61
  14.1 9.1 %collective-permute-start.4 = (bf16[64,4608]{1,0:T(8,128)(2,1)S(1)}, bf16[64,4608]{1,0:T(8,128)(2,1)S(1)}, u32[]{:S(2)}, u32[]{:S(2)}) collective-permute-start(bf16[64,4608]{1,0:T(8,128)(2,1)S(1)} %get-tuple-element.105), channel_id=1, source_target_pairs={{0,48},{8,24},{16,32},{24,8},{32,16},{40,56},{48,0},{56,40},{64,11... | collective-permute-start | bytes 1769480 | tf_op jit(solution)/shard_map/ppermute | solution.py:61
  15.4 14.1 %collective-permute-start.5 = (bf16[64,4608]{1,0:T(8,128)(2,1)S(1)}, bf16[64,4608]{1,0:T(8,128)(2,1)S(1)}, u32[]{:S(2)}, u32[]{:S(2)}) collective-permute-start(bf16[64,4608]{1,0:T(8,128)(2,1)S(1)} %get-tuple-element.104), channel_id=1, source_target_pairs={{0,48},{8,24},{16,32},{24,8},{32,16},{40,56},{48,0},{56,40},{64,11... | collective-permute-start | bytes 1769480 | tf_op jit(solution)/shard_map/ppermute | solution.py:61
  29.6 5.1 %collective-permute-start.6 = (bf16[128,4608]{1,0:T(8,128)(2,1)S(1)}, bf16[128,4608]{1,0:T(8,128)(2,1)S(1)}, u32[]{:S(2)}, u32[]{:S(2)}) collective-permute-start(bf16[128,4608]{1,0:T(8,128)(2,1)S(1)} %join.12.refs_1_), channel_id=1, source_target_pairs={{0,8},{8,0},{16,24},{24,16},{32,40},{40,32},{48,56},{56,48},{64,72... | collective-permute-start | bytes 3538952 | tf_op jit(solution)/shard_map/ppermute | solution.py:61
  32.1 9.9 %collective-permute-start.7 = (bf16[64,4608]{1,0:T(8,128)(2,1)S(1)}, bf16[64,4608]{1,0:T(8,128)(2,1)S(1)}, u32[]{:S(2)}, u32[]{:S(2)}) collective-permute-start(bf16[64,4608]{1,0:T(8,128)(2,1)S(1)} %join.10.refs_0_), channel_id=1, source_target_pairs={{0,16},{8,56},{16,0},{24,40},{32,48},{40,24},{48,32},{56,8},{64,80... | collective-permute-start | bytes 1769480 | tf_op jit(solution)/shard_map/ppermute | solution.py:61
  42.1 7.5 %collective-permute-start.8 = (bf16[128,4608]{1,0:T(8,128)(2,1)S(1)}, bf16[128,4608]{1,0:T(8,128)(2,1)S(1)}, u32[]{:S(2)}, u32[]{:S(2)}) collective-permute-start(bf16[128,4608]{1,0:T(8,128)(2,1)S(1)} %join.14.refs_0_), channel_id=1, source_target_pairs={{0,8},{8,0},{16,24},{24,16},{32,40},{40,32},{48,56},{56,48},{64,72... | collective-permute-start | bytes 3538952 | tf_op jit(solution)/shard_map/ppermute | solution.py:61
  42.3 15.4 %collective-permute-start.9 = (bf16[128,4608]{1,0:T(8,128)(2,1)S(1)}, bf16[128,4608]{1,0:T(8,128)(2,1)S(1)}, u32[]{:S(2)}, u32[]{:S(2)}) collective-permute-start(bf16[128,4608]{1,0:T(8,128)(2,1)S(1)} %join.14.refs_0_), channel_id=1, source_target_pairs={{0,48},{8,24},{16,32},{24,8},{32,16},{40,56},{48,0},{56,40},{64,11... | collective-permute-start | bytes 3538952 | tf_op jit(solution)/shard_map/ppermute | solution.py:61
  42.3 15.5 %collective-permute-start.10 = (s16[1024,512]{1,0:T(8,128)(2,1)S(1)}, s16[1024,512]{1,0:T(8,128)(2,1)S(1)}, u32[]{:S(2)}, u32[]{:S(2)}) collective-permute-start(s16[1024,512]{1,0:T(8,128)(2,1)S(1)} %gram.8), channel_id=1, source_target_pairs={{0,2},{1,3},{2,0},{3,1},{4,6},{5,7},{6,4},{7,5},{8,14},{9,15},{10,... | collective-permute-start | bytes 3145736 | tf_op jit(solution)/shard_map/ppermute | solution.py:70
  47.8 32.0 %collective-permute-start.11 = (s16[1024,512]{1,0:T(8,128)(2,1)S(1)}, s16[1024,512]{1,0:T(8,128)(2,1)S(1)}, u32[]{:S(2)}, u32[]{:S(2)}) collective-permute-start(s16[1024,512]{1,0:T(8,128)(2,1)S(1)} %gram.9), channel_id=1, source_target_pairs={{0,1},{1,0},{2,3},{3,2},{4,5},{5,4},{6,7},{7,6},{8,9},{9,8},{10,11... | collective-permute-start | bytes 3145736 | tf_op jit(solution)/shard_map/ppermute | solution.py:70
  70.2 25.3 %collective-permute-start.12 = (s16[1024,512]{1,0:T(8,128)(2,1)S(1)}, s16[1024,512]{1,0:T(8,128)(2,1)S(1)}, u32[]{:S(2)}, u32[]{:S(2)}) collective-permute-start(s16[1024,512]{1,0:T(8,128)(2,1)S(1)} %gram.12), channel_id=1, source_target_pairs={{0,1},{1,0},{2,3},{3,2},{4,5},{5,4},{6,7},{7,6},{8,9},{9,8},{10,11... | collective-permute-start | bytes 3145736 | tf_op jit(solution)/shard_map/ppermute | solution.py:70
  77.0 22.6 %collective-permute-start.13 = (s16[1024,512]{1,0:T(8,128)(2,1)S(1)}, s16[1024,512]{1,0:T(8,128)(2,1)S(1)}, u32[]{:S(2)}, u32[]{:S(2)}) collective-permute-start(s16[1024,512]{1,0:T(8,128)(2,1)S(1)} %gram.13), channel_id=1, source_target_pairs={{0,2},{1,3},{2,0},{3,1},{4,6},{5,7},{6,4},{7,5},{8,14},{9,15},{10,... | collective-permute-start | bytes 3145736 | tf_op jit(solution)/shard_map/ppermute | solution.py:70
  81.5 21.1 %collective-permute-start.14 = (s16[512,512]{1,0:T(8,128)(2,1)S(1)}, s16[512,512]{1,0:T(8,128)(2,1)S(1)}, u32[]{:S(2)}, u32[]{:S(2)}) collective-permute-start(s16[512,512]{1,0:T(8,128)(2,1)S(1)} %get-tuple-element.83), channel_id=1, source_target_pairs={{0,6},{1,7},{2,4},{3,5},{4,2},{5,3},{6,0},{7,1},{8,10},{9,11},{10,... | collective-permute-start | bytes 1572872 | tf_op jit(solution)/shard_map/ppermute | solution.py:70
  86.3 17.4 %collective-permute-start.15 = (s16[512,512]{1,0:T(8,128)(2,1)S(1)}, s16[512,512]{1,0:T(8,128)(2,1)S(1)}, u32[]{:S(2)}, u32[]{:S(2)}) collective-permute-start(s16[512,512]{1,0:T(8,128)(2,1)S(1)} %get-tuple-element.86), channel_id=1, source_target_pairs={{0,2},{1,3},{2,0},{3,1},{4,6},{5,7},{6,4},{7,5},{8,14},{9,15},{10,... | collective-permute-start | bytes 1572872 | tf_op jit(solution)/shard_map/ppermute | solution.py:70
  97.2 11.6 %collective-permute-start.16 = (s16[512,512]{1,0:T(8,128)(2,1)S(1)}, s16[512,512]{1,0:T(8,128)(2,1)S(1)}, u32[]{:S(2)}, u32[]{:S(2)}) collective-permute-start(s16[512,512]{1,0:T(8,128)(2,1)S(1)} %get-tuple-element.89), channel_id=1, source_target_pairs={{0,2},{1,3},{2,0},{3,1},{4,6},{5,7},{6,4},{7,5},{8,14},{9,15},{10,... | collective-permute-start | bytes 1572872 | tf_op jit(solution)/shard_map/ppermute | solution.py:70
  101.3 13.7 %collective-permute-start.17 = (s16[512,512]{1,0:T(8,128)(2,1)S(1)}, s16[512,512]{1,0:T(8,128)(2,1)S(1)}, u32[]{:S(2)}, u32[]{:S(2)}) collective-permute-start(s16[512,512]{1,0:T(8,128)(2,1)S(1)} %get-tuple-element.92), channel_id=1, source_target_pairs={{0,1},{1,0},{2,3},{3,2},{4,5},{5,4},{6,7},{7,6},{8,9},{9,8},{10,11... | collective-permute-start | bytes 1572872 | tf_op jit(solution)/shard_map/ppermute | solution.py:70
  109.9 6.3 %collective-permute-start.18 = (s16[256,512]{1,0:T(8,128)(2,1)S(1)}, s16[256,512]{1,0:T(8,128)(2,1)S(1)}, u32[]{:S(2)}, u32[]{:S(2)}) collective-permute-start(s16[256,512]{1,0:T(8,128)(2,1)S(1)} %get-tuple-element.94), channel_id=1, source_target_pairs={{0,6},{1,7},{2,4},{3,5},{4,2},{5,3},{6,0},{7,1},{8,10},{9,11},{10,... | collective-permute-start | bytes 786440 | tf_op jit(solution)/shard_map/ppermute | solution.py:70
  110.3 8.0 %collective-permute-start.20 = (s16[256,512]{1,0:T(8,128)(2,1)S(1)}, s16[256,512]{1,0:T(8,128)(2,1)S(1)}, u32[]{:S(2)}, u32[]{:S(2)}) collective-permute-start(s16[256,512]{1,0:T(8,128)(2,1)S(1)} %get-tuple-element.97), channel_id=1, source_target_pairs={{0,6},{1,7},{2,4},{3,5},{4,2},{5,3},{6,0},{7,1},{8,10},{9,11},{10,... | collective-permute-start | bytes 786440 | tf_op jit(solution)/shard_map/ppermute | solution.py:70
  111.5 8.0 %collective-permute-start.19 = (s16[256,512]{1,0:T(8,128)(2,1)S(1)}, s16[256,512]{1,0:T(8,128)(2,1)S(1)}, u32[]{:S(2)}, u32[]{:S(2)}) collective-permute-start(s16[256,512]{1,0:T(8,128)(2,1)S(1)} %get-tuple-element.96), channel_id=1, source_target_pairs={{0,1},{1,0},{2,3},{3,2},{4,5},{5,4},{6,7},{7,6},{8,9},{9,8},{10,11... | collective-permute-start | bytes 786440 | tf_op jit(solution)/shard_map/ppermute | solution.py:70
  116.1 5.6 %collective-permute-start.21 = (s16[256,512]{1,0:T(8,128)(2,1)S(1)}, s16[256,512]{1,0:T(8,128)(2,1)S(1)}, u32[]{:S(2)}, u32[]{:S(2)}) collective-permute-start(s16[256,512]{1,0:T(8,128)(2,1)S(1)} %get-tuple-element.100), channel_id=1, source_target_pairs={{0,6},{1,7},{2,4},{3,5},{4,2},{5,3},{6,0},{7,1},{8,10},{9,11},{10,... | collective-permute-start | bytes 786440 | tf_op jit(solution)/shard_map/ppermute | solution.py:70
  138.1 4.4 %collective-permute-start.27 = (f32[8,128]{1,0:T(8,128)S(1)}, f32[8,128]{1,0:T(8,128)S(1)}, u32[]{:S(2)}, u32[]{:S(2)}) collective-permute-start(f32[8,128]{1,0:T(8,128)S(1)} %add.38), channel_id=1, source_target_pairs={{0,65},{1,64},{2,67},{3,66},{4,69},{5,68},{6,71},{7,70},{8,73},{9,... | collective-permute-start | bytes 12296 | tf_op jit(solution)/shard_map/ppermute | solution.py:78
  142.5 10.6 %collective-permute-start.28 = (f32[8,128]{1,0:T(8,128)S(1)}, f32[8,128]{1,0:T(8,128)S(1)}, u32[]{:S(2)}, u32[]{:S(2)}) collective-permute-start(f32[8,128]{1,0:T(8,128)S(1)} %add.39), channel_id=1, source_target_pairs={{0,8},{8,0},{16,24},{24,16},{32,40},{40,32},{48,56},{56,48},{64,72... | collective-permute-start | bytes 12296 | tf_op jit(solution)/shard_map/ppermute | solution.py:61
  (8 other events, 52.8 us)
